TPU v7x, 32 devices: a whole 2x2x4 slice. The times are simulated.
32 devices in a mesh: run: 2 (over y), lon: 4 (over z), node: 2 (over x), lev: 2 (over core).
Axes of the slice: x: 2, y: 2, z: 4, core: 2. Of those that a mesh axis runs over, the one named last changes fastest.
Arguments:
- initial_state: float32 [8, 4, 96, 512], P(None, 'lev', 'run', 'lon'), parts along dimension 2, may hold values from -6 to 6
- node_states: float32 [8, 8, 4, 96, 512], P('node', None, 'lev', 'run', 'lon'), parts along dimension 3, may hold values from -6 to 6
- node_order: int32 [8], replicated, may hold values from 0 to 7, each once
- sector_depth: int32 [8, 96], P('node', 'run'), parts along dimension 1, may hold values from 0 to 2, as said below
- cell_offset: int32 [8, 96], P('node', 'run'), parts along dimension 1, may hold values from 2 to 127
- fraction: float32 [8, 96], P('node', 'run'), parts along dimension 1, may hold values from 0 to 1
- reaction_matrix: float32 [8, 8], replicated, may hold values from -2 to 2
- diffusivity: float32 [4], P('lev'), may hold values from 0.1 to 1
Outputs:
- new_states: float32 [8, 8, 4, 96, 512], P('node', None, 'lev', 'run', 'lon'), parts along dimension 3
There are 2 independent parts, one for each index of `run`. A program takes and returns all parts, laid end to end along the dimension named above; an argument that names none is the same for every part. Nothing has to cross between parts.
Inputs may be any that keep to these rules, and one draw needn't show every extreme that they name: `sector_depth`: rows among the 6 nearest either pole have depth 2 or more, all other rows depth 0 or 1; the rows at both poles have depth 2, the middle row depth 0.
All inputs are finite; a program needn't handle non-finite values.
Results may differ from a plain program's by a relative error of at most 0.0003.
Values sent between devices are 32-bit elements; how exact they have to be, the bound alone decides.
A program may use at most 128 MiB of HBM per device.

v0:
```python
import jax
import jax.numpy as jnp
import numpy as np
from jax import lax
from jax.sharding import PartitionSpec as P

NODES = 8


time_step = 0.5
lobatto_points = [
    -1.0,
    -0.8717401485096066,
    -0.5917001814331423,
    -0.2092992179024789,
    0.2092992179024789,
    0.5917001814331423,
    0.8717401485096066,
    1.0,
]


def padded_2(array, sides, width):
    for axis, dim in sides:
        size, length = (lax.axis_size(axis), array.shape[dim])
        up = [(i, (i + 1) % size) for i in range(size - 1)]
        down = [(j, i) for i, j in up]
        last = lax.slice_in_dim(array, length - width, length, axis=dim)
        first = lax.slice_in_dim(array, 0, width, axis=dim)
        before = lax.ppermute(last, axis, up)
        after = lax.ppermute(first, axis, down)
        array = jnp.concatenate([before, array, after], axis=dim)
    return array


def passed_along(array, axis, by):
    length = lax.axis_size(axis)
    return lax.ppermute(array, axis, [(i, (i + by) % length) for i in range(length)])


def lobatto_table():
    points = [(value + 1.0) / 2.0 for value in lobatto_points]
    result_rows = [[0.0] * 8 for m in range(8)]
    for j in range(8):
        poly_coeffs = [1.0]
        for k in range(8):
            if k != j:
                factor = 1.0 / (points[j] - points[k])
                grown = [0.0] * (len(poly_coeffs) + 1)
                for i in range(len(poly_coeffs)):
                    grown[i + 1] = grown[i + 1] + poly_coeffs[i] * factor
                    grown[i] = grown[i] - poly_coeffs[i] * points[k] * factor
                poly_coeffs = grown
        for m in range(8):
            total_value = 0.0
            for i in range(len(poly_coeffs)):
                total_value = total_value + poly_coeffs[i] * points[m] ** (i + 1) / (i + 1)
            result_rows[m][j] = total_value
    return np.array(result_rows)


def cubic_weights(fraction):
    return (
        -fraction * (fraction - 1.0) * (fraction - 2.0) / 6.0,
        (fraction + 1.0) * (fraction - 1.0) * (fraction - 2.0) / 2.0,
        -(fraction + 1.0) * fraction * (fraction - 2.0) / 2.0,
        (fraction + 1.0) * fraction * (fraction - 1.0) / 6.0,
    )


def section_matrix(node_order):
    onehot = (node_order[:, None] == jnp.arange(NODES, dtype=jnp.int32)[None, :]).astype(
        jnp.float32
    )
    quad_values = jnp.asarray(lobatto_table(), jnp.float32)
    left = jnp.dot(onehot, quad_values, precision=lax.Precision.HIGHEST)
    return jnp.dot(left, onehot.T, precision=lax.Precision.HIGHEST)


def tendency_of(states, reaction_matrix, diffusivity):
    level_count = states.shape[2]
    padded = padded_2(states, (("lev", 2),), 1)
    level_pos = lax.axis_index("lev")
    level_last = lax.axis_size("lev") - 1
    below = padded[:, :, :level_count]
    above = padded[:, :, 2:]
    bottom_level = jnp.where(level_pos == 0, states[:, :, :1], below[:, :, :1])
    below = jnp.concatenate([bottom_level, below[:, :, 1:]], axis=2)
    top_level = jnp.where(
        level_pos == level_last, states[:, :, level_count - 1 :], above[:, :, level_count - 1 :]
    )
    above = jnp.concatenate([above[:, :, : level_count - 1], top_level], axis=2)
    curvature = above - 2.0 * states + below
    reaction = jnp.einsum(
        "ts,mslyx->mtlyx", reaction_matrix, jnp.tanh(states), precision=lax.Precision.HIGHEST
    )
    return reaction + diffusivity[None, None, :, None, None] * curvature


def cut_window(field, start, length):
    return lax.dynamic_slice_in_dim(field, start, length, 2)


def advect_rows(sectioned, sector_depth, cell_offset, fraction):
    sector_cells = sectioned.shape[4]
    reach_max = min(4, lax.axis_size("lon") - 2) + 1
    depth_cells = sector_depth[:, None, None, :, None]
    nearer = jnp.where(depth_cells == 0, sectioned, 0.0)
    farther = jnp.zeros_like(sectioned)
    previous = sectioned
    for distance in range(1, reach_max + 1):
        source = previous
        arrived = passed_along(source, "lon", 1)
        previous = arrived
        nearer = nearer + jnp.where(depth_cells == distance, arrived, 0.0)
        farther = farther + jnp.where(depth_cells + 1 == distance, arrived, 0.0)
    window = jnp.concatenate([farther, nearer], axis=4)
    starts = sector_cells - cell_offset - 1
    cut_len = sector_cells + 3
    per_row = jax.vmap(cut_window, in_axes=(2, 0, None), out_axes=2)
    per_slot = jax.vmap(per_row, in_axes=(0, 0, None), out_axes=0)
    pieces = per_slot(window, starts, cut_len)
    coeffs = cubic_weights(fraction)
    result = jnp.zeros_like(sectioned)
    for stencil in range(4):
        result = (
            result
            + coeffs[stencil][:, None, None, :, None]
            * pieces[:, :, :, :, stencil : stencil + sector_cells]
        )
    return result


def shards(
    initial_state,
    node_states,
    node_order,
    sector_depth,
    cell_offset,
    fraction,
    reaction_matrix,
    diffusivity,
):
    slots = node_states.shape[0]
    weights = section_matrix(node_order)
    node_pos = lax.axis_index("node")
    tendency = tendency_of(node_states, reaction_matrix, diffusivity)
    own_rows = lax.dynamic_slice_in_dim(weights, node_pos * slots, slots, 0)
    integral = jnp.einsum(
        "mj,jtlyx->mtlyx",
        own_rows,
        lax.all_gather(tendency, "node", axis=0, tiled=True),
        precision=lax.Precision.HIGHEST,
    )
    sectioned = initial_state[None] + time_step * integral
    return advect_rows(sectioned, sector_depth, cell_offset, fraction)


def solution(mesh):
    in_specs = (
        P(None, "lev", "run", "lon"),
        P("node", None, "lev", "run", "lon"),
        P(),
        P("node", "run"),
        P("node", "run"),
        P("node", "run"),
        P(),
        P("lev"),
    )
    out_specs = P("node", None, "lev", "run", "lon")
    return jax.shard_map(shards, mesh=mesh, in_specs=in_specs, out_specs=out_specs, check_vma=False)
```

profile of v0, /device:TPU:0, one launch (start us, length us, event | category | flops | bytes accessed | tf_op | source)
XLA Modules:
  0.0 328.9 jit_solution(18254070785637578791)
XLA Ops:
  6.5 2.8 fusion.31
  9.3 1.3 collective-permute-start
  10.6 4.8 %collective-permute-start.1 = (f32[4,8,1,48,128]{4,3,2,1,0:T(8,128)}, f32[4,8,1,48,128]{4,3,2,1,0:T(8,128)}, u32[]{:S(2)}, u32[]{:S(2)}) collective-permute-start(f32[4,8,1,48,128]{4,3,2,1,0:T(8,128)} %get-tuple-element.9), channel_id=1, source_target_pairs={{0,1},{2,3},{4,5},{6,7},{8,9},{10,11},{12,13},{14,15},{16,17},{18,... | collective-permute-start | bytes 2359304 | tf_op jit(solution)/shard_map/ppermute | solution.py:30
  15.4 0.2 tanh.3
  15.6 2.4 fusion.8
  18.1 1.4 broadcast_select_fusion
  19.5 3.2 fusion.7
  22.7 0.6 copy-done.8
  23.4 0.2 fusion.14
  23.6 0.2 fusion.13
  23.8 46.7 %all-gather.2.cloned.1.call-done = f32[8,8,2,48,128]{4,3,2,1,0:T(8,128)} async-done(((f32[4,8,2,48,128]{4,3,2,1,0:T(8,128)}), f32[8,8,2,48,128]{4,3,2,1,0:T(8,128)}) %all-gather.2.cloned.1.call-update) | async-done | bytes 3145744 | tf_op jit(solution)/shard_map/all_gather | solution.py:152
  70.5 6.5 %multiply_add_fusion = f32[4,8,2,48,128]{4,0,3,2,1:T(4,128)S(1)} fusion(f32[8,8,2,48,128]{4,3,2,1,0:T(8,128)} %all-gather.2.cloned.1.call-done, f32[8,2,48,128]{3,2,1,0:T(8,128)S(1)} %copy-done.3, f32[8,8]{1,0:T(8,128)S(1)} %fusion.13, s32[]{:T(128)S(6)} %select_n.42), kind=kOutput, calls=%fused_computation.19 | convolution fusion | flops 38535168 | bytes 5113860 | tf_op jit(solution)/shard_map/mj,jtlyx->mtlyx/dot_general | solution.py:149
  77.0 1.5 collective-permute-start.2
  78.6 36.4 %collective-permute-done.2 = f32[4,8,2,48,128]{4,0,3,2,1:T(4,128)S(1)} collective-permute-done((f32[4,8,2,48,128]{4,0,3,2,1:T(4,128)S(1)}, f32[4,8,2,48,128]{4,0,3,2,1:T(4,128)S(1)}, u32[]{:S(2)}, u32[]{:S(2)}) %collective-permute-start.2) | collective-permute-done | bytes 1572896 | tf_op jit(solution)/shard_map/ppermute | solution.py:38
  115.0 37.2 %collective-permute-done.3 = f32[4,8,2,48,128]{4,0,3,2,1:T(4,128)} collective-permute-done((f32[4,8,2,48,128]{4,0,3,2,1:T(4,128)S(1)}, f32[4,8,2,48,128]{4,0,3,2,1:T(4,128)}, u32[]{:S(2)}, u32[]{:S(2)}) %collective-permute-start.3) | collective-permute-done | bytes 1572896 | tf_op jit(solution)/shard_map/ppermute | solution.py:38
  152.2 0.1 copy.22
  152.3 0.1 copy.24
  153.1 35.6 %collective-permute-done.4 = f32[4,8,2,48,128]{4,0,3,2,1:T(4,128)} collective-permute-done((f32[4,8,2,48,128]{4,0,3,2,1:T(4,128)}, f32[4,8,2,48,128]{4,0,3,2,1:T(4,128)}, u32[]{:S(2)}, u32[]{:S(2)}) %collective-permute-start.4) | collective-permute-done | bytes 1572896 | tf_op jit(solution)/shard_map/ppermute | solution.py:38
  188.6 3.9 %select_add_fusion.1 = (f32[4,8,2,48,128]{4,0,3,2,1:T(4,128)S(1)}, f32[4,8,2,48,128]{4,0,3,2,1:T(4,128)S(1)}) fusion(f32[4,8,2,48,128]{4,0,3,2,1:T(4,128)} %collective-permute-done.4, f32[4,8,2,48,128]{4,0,3,2,1:T(4,128)} %collective-permute-done.3, f32[4,8,2,48,128]{4,0,3,2,1:T(4,128)S(1)} %collective-permute-done.2, pred[4,48]{0,1:T(8,128)(4,1)S(1)} %copy.25, ...), kind=kLoop, calls=%fused_computation.18 | loop fusion | flops 4718592 | bytes 9438528 | tf_op jit(solution)/shard_map/add | solution.py:116
  192.5 0.8 maximum_bitcast_fusion
  193.3 52.7 %copy.30 = f32[4,48,8,2,256]{2,3,1,0,4:T(2,128)} copy(f32[4,48,8,2,256]{4,0,1,3,2:T(4,128)S(1)} %maximum_bitcast_fusion) | data formatting | bytes 6291456 | tf_op jit(solution)/shard_map/vmap(vmap())/transpose | solution.py:101
  246.0 36.2 %gather_fusion = f32[192,8,2,131]{1,2,3,0:T(2,128)} fusion(f32[4,48,8,2,256]{2,3,1,0,4:T(2,128)} %copy.30, s32[192]{0:T(256)S(1)} %reshape.22), kind=kCustom, calls=%fused_computation | custom fusion | bytes 3223296 | tf_op jit(solution)/shard_map/vmap(vmap())/gather | solution.py:101
  282.2 37.2 %copy.31 = f32[4,48,8,2,131]{4,1,3,2,0:T(8,128)S(1)} copy(f32[4,48,8,2,131]{2,3,4,1,0:T(2,128)} %bitcast.24) | data formatting | bytes 3219456 | tf_op jit(solution)/shard_map/vmap(vmap())/gather | solution.py:101
  319.5 2.5 fusion.2
  (34 shorter events, 0.8 us)
Async XLA Ops:
  6.5 9.1 %copy-start = (f32[8,8]{1,0:T(8,128)S(1)}, f32[8,8]{1,0:T(8,128)}, u32[]{:S(2)}) copy-start(f32[8,8]{1,0:T(8,128)} %param.15) | copy-start | bytes 772
  6.5 8.9 %copy-start.2 = (f32[4,8,2,48,128]{4,3,2,1,0:T(8,128)S(1)}, f32[4,8,2,48,128]{4,3,2,1,0:T(8,128)}, u32[]{:S(2)}) copy-start(f32[4,8,2,48,128]{4,3,2,1,0:T(8,128)} %param.10) | copy-start | bytes 4718596
  6.5 64.0 %all-gather.2.cloned.1.call-start = ((), (), s32[]{:S(2)}) async-start(), calls=%async_computation | async-start | bytes 4718592 | tf_op jit(solution)/shard_map/all_gather | solution.py:152
  9.3 8.8 %collective-permute-start = (f32[4,8,1,48,128]{4,3,2,1,0:T(8,128)}, f32[4,8,1,48,128]{4,3,2,1,0:T(8,128)}, u32[]{:S(2)}, u32[]{:S(2)}) collective-permute-start(f32[4,8,1,48,128]{4,3,2,1,0:T(8,128)} %get-tuple-element.10), channel_id=1, source_target_pairs={{1,0},{3,2},{5,4},{7,6},{9,8},{11,10},{13,12},{15,14},{17,16},{19,... | collective-permute-start | bytes 2359304 | tf_op jit(solution)/shard_map/ppermute | solution.py:31
  10.6 7.5 %collective-permute-start.1 = (f32[4,8,1,48,128]{4,3,2,1,0:T(8,128)}, f32[4,8,1,48,128]{4,3,2,1,0:T(8,128)}, u32[]{:S(2)}, u32[]{:S(2)}) collective-permute-start(f32[4,8,1,48,128]{4,3,2,1,0:T(8,128)} %get-tuple-element.9), channel_id=1, source_target_pairs={{0,1},{2,3},{4,5},{6,7},{8,9},{10,11},{12,13},{14,15},{16,17},{18,... | collective-permute-start | bytes 2359304 | tf_op jit(solution)/shard_map/ppermute | solution.py:30
  18.1 1.5 copy-start.7
  22.7 0.7 copy-start.8
  22.7 0.7 copy-start.9
  22.7 47.8 %copy-start.3 = (f32[8,2,48,128]{3,2,1,0:T(8,128)S(1)}, f32[8,2,48,128]{3,2,1,0:T(8,128)}, u32[]{:S(2)}) copy-start(f32[8,2,48,128]{3,2,1,0:T(8,128)} %param.9) | copy-start | bytes 1179652
  23.8 128.4 %copy-start.6 = (s32[4,48]{1,0:T(4,128)S(1)}, s32[4,48]{1,0:T(4,128)}, u32[]{:S(2)}) copy-start(s32[4,48]{1,0:T(4,128)} %param.12) | copy-start | bytes 2308
  23.8 129.2 %copy-start.5 = (s32[4,48]{1,0:T(4,128)S(1)}, s32[4,48]{1,0:T(4,128)}, u32[]{:S(2)}) copy-start(s32[4,48]{1,0:T(4,128)} %param.13) | copy-start | bytes 2308
  23.8 129.3 %copy-start.4 = (f32[4,48]{1,0:T(4,128)S(1)}, f32[4,48]{1,0:T(4,128)}, u32[]{:S(2)}) copy-start(f32[4,48]{1,0:T(4,128)} %param.14) | copy-start | bytes 2308
  77.0 38.0 %collective-permute-start.2 = (f32[4,8,2,48,128]{4,0,3,2,1:T(4,128)S(1)}, f32[4,8,2,48,128]{4,0,3,2,1:T(4,128)S(1)}, u32[]{:S(2)}, u32[]{:S(2)}) collective-permute-start(f32[4,8,2,48,128]{4,0,3,2,1:T(4,128)S(1)} %multiply_add_fusion), channel_id=1, source_target_pairs={{0,4},{4,8},{8,12},{12,0},{1,5},{5,9},{9,13},{13,1},{2,6},{6,10},{... | collective-permute-start | bytes 4718600 | tf_op jit(solution)/shard_map/ppermute | solution.py:38
  115.0 37.2 %collective-permute-start.3 = (f32[4,8,2,48,128]{4,0,3,2,1:T(4,128)S(1)}, f32[4,8,2,48,128]{4,0,3,2,1:T(4,128)}, u32[]{:S(2)}, u32[]{:S(2)}) collective-permute-start(f32[4,8,2,48,128]{4,0,3,2,1:T(4,128)S(1)} %collective-permute-done.2), channel_id=1, source_target_pairs={{0,4},{4,8},{8,12},{12,0},{1,5},{5,9},{9,13},{13,1},{2,6},{6,10},{... | collective-permute-start | bytes 4718600 | tf_op jit(solution)/shard_map/ppermute | solution.py:38
  152.2 36.5 %collective-permute-start.4 = (f32[4,8,2,48,128]{4,0,3,2,1:T(4,128)}, f32[4,8,2,48,128]{4,0,3,2,1:T(4,128)}, u32[]{:S(2)}, u32[]{:S(2)}) collective-permute-start(f32[4,8,2,48,128]{4,0,3,2,1:T(4,128)} %collective-permute-done.3), channel_id=1, source_target_pairs={{0,4},{4,8},{8,12},{12,0},{1,5},{5,9},{9,13},{13,1},{2,6},{6,10},{... | collective-permute-start | bytes 4718600 | tf_op jit(solution)/shard_map/ppermute | solution.py:38
  319.4 2.6 copy-start.1
Sparse Core Ops, SparseCore 0:
  22.8 47.6 all-gather.1
where the time goes:
time: 330 us; the launch traced here: 329 us
  waiting for transfers between devices  156 us (47%)
  local copies, waits for them, and re-layouts  131 us (40%)
  between operations  13.5 us (4%)
  other arithmetic  11.8 us (4%)
  matrix products  9.28 us (3%)
  starting transfers between devices  7.63 us (2%)
    ppermute x3, waiting for transfers between devices, passed_along(): lax.ppermute(array, axis, [(i, (i + by) % length) for i in range(length)])  109 us
    gather x3, local copies, waits for them, and re-layouts, cut_window(): return lax.dynamic_slice_in_dim(field, start, length, 2)  73.5 us
    transpose x1, local copies, waits for them, and re-layouts, cut_window(): return lax.dynamic_slice_in_dim(field, start, length, 2)  52.7 us
    all_gather x1, waiting for transfers between devices, shards(): lax.all_gather(tendency, 'node', axis=0, tiled=True)  46.7 us
  transfers between devices with their start and end apart: 6, of which 4 were waited for; matrix products, arithmetic and copies ran while one was open for 1% of the time, Pallas kernels for 0%

commit v1 on v0

--- a/solution.py
+++ b/solution.py
@@ -2,6 +2,8 @@
 import jax.numpy as jnp
 import numpy as np
 from jax import lax
+from jax.experimental import pallas as pl
+from jax.experimental.pallas import tpu as pltpu
 from jax.sharding import PartitionSpec as P
 
 NODES = 8
@@ -97,8 +99,13 @@
     return reaction + diffusivity[None, None, :, None, None] * curvature
 
 
-def cut_window(field, start, length):
-    return lax.dynamic_slice_in_dim(field, start, length, 2)
+def shifted_window(window, starts, length):
+    starts = starts[:, None, None, :, None]
+    bit = 1
+    while bit < length:
+        window = jnp.where((starts & bit) != 0, jnp.roll(window, -bit, axis=4), window)
+        bit *= 2
+    return window
 
 
 def advect_rows(sectioned, sector_depth, cell_offset, fraction):
@@ -116,10 +123,7 @@
         farther = farther + jnp.where(depth_cells + 1 == distance, arrived, 0.0)
     window = jnp.concatenate([farther, nearer], axis=4)
     starts = sector_cells - cell_offset - 1
-    cut_len = sector_cells + 3
-    per_row = jax.vmap(cut_window, in_axes=(2, 0, None), out_axes=2)
-    per_slot = jax.vmap(per_row, in_axes=(0, 0, None), out_axes=0)
-    pieces = per_slot(window, starts, cut_len)
+    pieces = shifted_window(window, starts, sector_cells)
     coeffs = cubic_weights(fraction)
     result = jnp.zeros_like(sectioned)
     for stencil in range(4):
@@ -156,6 +160,324 @@
     return advect_rows(sectioned, sector_depth, cell_offset, fraction)
 
 
+MESH = pl.DeviceIdType.MESH
+ROWS = 8
+
+
+def sweep_kernel(
+    order_ref,
+    quad_ref,
+    reaction_ref,
+    diff_ref,
+    init_ref,
+    states_ref,
+    depth_ref,
+    offset_ref,
+    frac_ref,
+    out_ref,
+    edge,
+    part,
+    part_in,
+    sect,
+    far_out,
+    far_in,
+    row_depth,
+    row_offset,
+    row_frac,
+    edge_s,
+    edge_r,
+    part_s,
+    part_r,
+    sect_s,
+    sect_r,
+    far_s,
+    far_r,
+):
+    slots, tracers, _, nlat, cells = states_ref.shape
+    blocks = nlat // ROWS
+    chunks = 2 * blocks
+    lev = lax.axis_index("lev")
+    node = lax.axis_index("node")
+    lon = lax.axis_index("lon")
+    half = lon // 2
+    par = lon % 2
+    mate = half * 2 + (1 - par)
+    middle = (lon == 1) | (lon == 2)
+
+    barrier = pltpu.get_barrier_semaphore()
+    pl.semaphore_signal(barrier, inc=1, device_id={"lev": 1 - lev}, device_id_type=MESH)
+    pl.semaphore_signal(barrier, inc=1, device_id={"node": 1 - node}, device_id_type=MESH)
+    for step in range(1, 4):
+        pl.semaphore_signal(
+            barrier, inc=1, device_id={"lon": (lon + step) % 4}, device_id_type=MESH
+        )
+    pl.semaphore_wait(barrier, 5)
+
+    def edge_copy(block):
+        rows = pl.ds(pl.multiple_of(block * ROWS, ROWS), ROWS)
+        return pltpu.make_async_remote_copy(
+            src_ref=states_ref.at[:, :, 1 - lev, rows, :],
+            dst_ref=edge.at[:, :, rows, :],
+            send_sem=edge_s.at[block],
+            recv_sem=edge_r.at[block],
+            device_id={"lev": 1 - lev},
+            device_id_type=MESH,
+        )
+
+    def part_copy(c):
+        return pltpu.make_async_remote_copy(
+            src_ref=part.at[c],
+            dst_ref=part_in.at[c],
+            send_sem=part_s.at[c],
+            recv_sem=part_r.at[c],
+            device_id={"node": 1 - node},
+            device_id_type=MESH,
+        )
+
+    def sect_copy(c):
+        return pltpu.make_async_remote_copy(
+            src_ref=sect.at[par, c],
+            dst_ref=sect.at[par, c],
+            send_sem=sect_s.at[c],
+            recv_sem=sect_r.at[c],
+            device_id={"lon": mate},
+            device_id_type=MESH,
+        )
+
+    def far_copy(which, c):
+        return pltpu.make_async_remote_copy(
+            src_ref=far_out.at[which, c],
+            dst_ref=far_in.at[c],
+            send_sem=far_s.at[which, c],
+            recv_sem=far_r.at[c],
+            device_id={"lon": (1 - half) * 2 + which},
+            device_id_type=MESH,
+        )
+
+    def start_edge(block, carry):
+        edge_copy(block).start()
+        return carry
+
+    lax.fori_loop(0, blocks, start_edge, 0)
+
+    diagonal = lax.broadcasted_iota(jnp.int32, (nlat, nlat), 0) == lax.broadcasted_iota(
+        jnp.int32, (nlat, nlat), 1
+    )
+    for a in range(slots):
+        for source, target in (
+            (depth_ref, row_depth),
+            (offset_ref, row_offset),
+            (frac_ref, row_frac),
+        ):
+            line = jnp.broadcast_to(source[a : a + 1, :], (nlat, nlat)).astype(jnp.float32)
+            column = jnp.sum(jnp.where(diagonal, line, 0.0), axis=1, keepdims=True)
+            target[a] = jnp.broadcast_to(column, (nlat, cells)).astype(target.dtype)
+
+    def place(c):
+        block = c // 2
+        level = jnp.where(c % 2 == 0, lev, 1 - lev)
+        return block, level, pl.ds(pl.multiple_of(block * ROWS, ROWS), ROWS)
+
+    def tendencies(c):
+        block, level, rows = place(c)
+        outer = c % 2 == 0
+
+        @pl.when(jnp.logical_not(outer))
+        def _():
+            edge_copy(block).wait_recv()
+
+        coefficient = diff_ref[level]
+
+        def body(outer):
+            tend = []
+            for m in range(slots):
+                own = [states_ref[m, t, level, rows, :] for t in range(tracers)]
+                acts = [jnp.tanh(x) for x in own]
+                row = []
+                for t in range(tracers):
+                    beyond = own[t] if outer else edge[m, t, rows, :]
+                    near = states_ref[m, t, 1 - level, rows, :]
+                    value = coefficient * (near - 2.0 * own[t] + beyond)
+                    for s in range(tracers):
+                        value = value + reaction_ref[t, s] * acts[s]
+                    row.append(value)
+                tend.append(row)
+            for target in range(2):
+                group = jnp.where(target == 0, 1 - node, node)
+                for a in range(slots):
+                    to = order_ref[group * slots + a]
+                    w = [
+                        time_step * quad_ref[to, order_ref[node * slots + m]]
+                        for m in range(slots)
+                    ]
+                    for t in range(tracers):
+                        value = w[0] * tend[0][t]
+                        for m in range(1, slots):
+                            value = value + w[m] * tend[m][t]
+                        if target == 0:
+                            part[c, a, t] = value
+                        else:
+                            sect[par, c, a, t] = init_ref[t, level, rows, :] + value
+
+        pl.when(outer)(lambda: body(True))
+        pl.when(jnp.logical_not(outer))(lambda: body(False))
+        part_copy(c).start()
+
+    def section(c):
+        part_copy(c).wait_recv()
+        sect[par, c] = sect[par, c] + part_in[c]
+        sect_copy(c).start()
+
+    def interpolate(c):
+        block, level, rows = place(c)
+        sect_copy(c).wait_recv()
+        lanes = lax.broadcasted_iota(jnp.int32, (ROWS, cells), 1)
+
+        def per_slot(a, carry):
+            depth = row_depth[a, rows, :]
+            offset = row_offset[a, rows, :]
+            coeffs = cubic_weights(row_frac[a, rows, :])
+            picks = [(lanes - offset + k) & (cells - 1) for k in range(-1, 3)]
+            reach = [
+                jnp.where(lanes >= offset - k, depth, depth + 1) for k in range(-1, 3)
+            ]
+
+            def weights_of(u):
+                rel = [(u - e) & 3 for e in reach]
+                return [
+                    [jnp.where(r == source, w, 0.0) for r, w in zip(rel, coeffs)]
+                    for source in range(2)
+                ]
+
+            def total(taps, weights):
+                value = None
+                for source in range(2):
+                    for k in range(4):
+                        term = weights[source][k] * taps[source][k]
+                        value = term if value is None else value + term
+                return value
+
+            def run(with_far):
+                own = weights_of(par)
+                far = [weights_of(2), weights_of(3)] if with_far else []
+                for t in range(tracers):
+                    fields = [sect[source, c, a, t] for source in range(2)]
+                    taps = [
+                        [
+                            jnp.take_along_axis(f, p, axis=1, mode="promise_in_bounds")
+                            for p in picks
+                        ]
+                        for f in fields
+                    ]
+                    out_ref[a, t, level, rows, :] = total(taps, own)
+                    for which, weights in enumerate(far):
+                        far_out[which, c, a, t] = total(taps, weights)
+
+            pl.when(middle)(lambda: run(True))
+            pl.when(jnp.logical_not(middle))(lambda: run(False))
+            return carry
+
+        lax.fori_loop(0, slots, per_slot, 0)
+
+        @pl.when(middle)
+        def _():
+            far_copy(0, c).start()
+            far_copy(1, c).start()
+
+    def step(i, carry):
+        pl.when(i < chunks)(lambda: tendencies(i))
+        pl.when((i >= 1) & (i < chunks + 1))(lambda: section(i - 1))
+        pl.when(i >= 2)(lambda: interpolate(i - 2))
+        return carry
+
+    lax.fori_loop(0, chunks + 2, step, 0)
+
+    def finish(c, carry):
+        block, level, rows = place(c)
+        far_copy(0, c).wait_recv()
+        out_ref[:, :, level, rows, :] = out_ref[:, :, level, rows, :] + far_in[c]
+        return carry
+
+    lax.fori_loop(0, chunks, finish, 0)
+
+    def drain(c, carry):
+        part_copy(c).wait_send()
+        sect_copy(c).wait_send()
+
+        @pl.when(middle)
+        def _():
+            far_copy(0, c).wait_send()
+            far_copy(1, c).wait_send()
+
+        return carry
+
+    lax.fori_loop(0, chunks, drain, 0)
+
+    def drain_edge(block, carry):
+        edge_copy(block).wait_send()
+        return carry
+
+    lax.fori_loop(0, blocks, drain_edge, 0)
+
+
+def kernel_shards(
+    initial_state,
+    node_states,
+    node_order,
+    sector_depth,
+    cell_offset,
+    fraction,
+    reaction_matrix,
+    diffusivity,
+):
+    slots, tracers, levels, nlat, cells = node_states.shape
+    blocks = nlat // ROWS
+    chunks = 2 * blocks
+    piece = (slots, tracers, ROWS, cells)
+    smem = pl.BlockSpec(memory_space=pltpu.SMEM)
+    vmem = pl.BlockSpec(memory_space=pltpu.VMEM)
+    f32 = jnp.float32
+    dma = pltpu.SemaphoreType.DMA
+    return pl.pallas_call(
+        sweep_kernel,
+        out_shape=jax.ShapeDtypeStruct(node_states.shape, f32),
+        in_specs=[smem] * 4 + [vmem] * 5,
+        out_specs=vmem,
+        scratch_shapes=[
+            pltpu.VMEM((slots, tracers, nlat, cells), f32),
+            pltpu.VMEM((chunks, *piece), f32),
+            pltpu.VMEM((chunks, *piece), f32),
+            pltpu.VMEM((2, chunks, *piece), f32),
+            pltpu.VMEM((2, chunks, *piece), f32),
+            pltpu.VMEM((chunks, *piece), f32),
+            pltpu.VMEM((slots, nlat, cells), jnp.int32),
+            pltpu.VMEM((slots, nlat, cells), jnp.int32),
+            pltpu.VMEM((slots, nlat, cells), f32),
+            dma((blocks,)),
+            dma((blocks,)),
+            dma((chunks,)),
+            dma((chunks,)),
+            dma((chunks,)),
+            dma((chunks,)),
+            dma((2, chunks)),
+            dma((chunks,)),
+        ],
+        compiler_params=pltpu.CompilerParams(
+            collective_id=0, has_side_effects=True, vmem_limit_bytes=40 * 1024 * 1024
+        ),
+    )(
+        node_order,
+        jnp.asarray(lobatto_table(), f32),
+        reaction_matrix,
+        diffusivity,
+        initial_state,
+        node_states,
+        sector_depth,
+        cell_offset,
+        fraction,
+    )
+
+
 def solution(mesh):
     in_specs = (
         P(None, "lev", "run", "lon"),
@@ -168,4 +490,7 @@
         P("lev"),
     )
     out_specs = P("node", None, "lev", "run", "lon")
-    return jax.shard_map(shards, mesh=mesh, in_specs=in_specs, out_specs=out_specs, check_vma=False)
+    sizes = dict(mesh.shape)
+    small = sizes["lon"] == 4 and sizes["node"] == 2 and sizes["lev"] == 2
+    body = kernel_shards if small else shards
+    return jax.shard_map(body, mesh=mesh, in_specs=in_specs, out_specs=out_specs, check_vma=False)

time: 330 us -> 92.4 us (0.28)
  waiting for transfers between devices: 156 us -> 0 us
  local copies, waits for them, and re-layouts: 131 us -> 8.27 us
  Pallas kernels: 0 us -> 83.8 us
  between operations: 13.5 us -> 0.02 us
  other arithmetic: 11.8 us -> 0 us
  matrix products: 9.28 us -> 0 us
  starting transfers between devices: 7.63 us -> 0 us
    ppermute x5 -> x0, waiting for transfers between devices: 109 us -> none  [the longest x3 109 us: passed_along(): lax.ppermute(array, axis, [(i, (i + by) % length) for i in range(length)])]
    pallas_call x0 -> x1, Pallas kernels: none -> 83.8 us  [kernel_shards(): pl.pallas_call(sweep_kernel, out_shape=jax.ShapeDtypeStruct(node_states.s...]
    gather x3 -> x0, local copies, waits for them, and re-layouts: 73.5 us -> none  [cut_window(): return lax.dynamic_slice_in_dim(field, start, length, 2)]
    transpose x1 -> x0, local copies, waits for them, and re-layouts: 52.7 us -> none  [cut_window(): return lax.dynamic_slice_in_dim(field, start, length, 2)]
    all_gather x1 -> x0, waiting for transfers between devices: 46.7 us -> none  [shards(): lax.all_gather(tendency, 'node', axis=0, tiled=True)]
    add x3 -> x0, other arithmetic: 9.57 us -> none  [the longest x1 3.86 us: advect_rows(): farther = farther + jnp.where(depth_cells + 1 == distance, arrived, 0.0)]
    dot_general x4 -> x0, matrix products: 9.28 us -> none  [the longest x1 6.51 us: shards(): jnp.einsum('mj,jtlyx->mtlyx', own_rows, lax.all_gather(tendency, 'node',...]
    ppermute x5 -> x0, starting transfers between devices: 7.63 us -> none  [the longest x1 4.8 us: padded_2(): before = lax.ppermute(last, axis, up)]
  transfers between devices with their start and end apart: 6 -> 0, of which waited for: 4 -> 0; matrix products, arithmetic and copies ran while one was open for 1% -> 0% of each run, Pallas kernels for 0% -> 0%
where the time goes in v1:
time: 92.4 us; the launch traced here: 92 us
  Pallas kernels  83.8 us (91%)
  local copies, waits for them, and re-layouts  8.27 us (9%)
    pallas_call x1, Pallas kernels, kernel_shards(): pl.pallas_call(sweep_kernel, out_shape=jax.ShapeDtypeStruct(node_states.s...  83.8 us
    unnamed x19, local copies, waits for them, and re-layouts  8.27 us

profile of v1, /device:TPU:0, one launch (start us, length us, event | category | flops | bytes accessed | tf_op | source)
XLA Modules:
  0.0 92.0 jit_solution(7313699055676403671)
XLA Ops:
  0.0 0.0 copy-start
  0.0 1.4 %copy-done = f32[4,8,2,48,128]{4,3,2,1,0:T(8,128)S(1)} copy-done((f32[4,8,2,48,128]{4,3,2,1,0:T(8,128)S(1)}, f32[4,8,2,48,128]{4,3,2,1,0:T(8,128)}, u32[]{:S(2)}) %copy-start) | copy-done | bytes 1572888
  1.4 0.0 copy-start.1
  1.4 1.0 %copy-done.1 = f32[8,2,48,128]{3,2,1,0:T(8,128)S(1)} copy-done((f32[8,2,48,128]{3,2,1,0:T(8,128)S(1)}, f32[8,2,48,128]{3,2,1,0:T(8,128)}, u32[]{:S(2)}) %copy-start.1) | copy-done | bytes 393240
  2.4 0.0 copy-start.2
  2.4 0.7 copy-done.2
  3.1 0.0 copy-start.3
  3.1 0.7 copy-done.3
  3.8 0.0 copy-start.4
  3.8 0.7 copy-done.4
  4.5 0.0 copy-start.5
  4.5 0.7 copy-done.5
  5.1 0.0 copy-start.6
  5.1 0.7 copy-done.6
  5.8 0.0 copy-start.7
  5.8 0.7 copy-done.7
  6.5 0.0 copy-start.8
  6.5 0.7 copy-done.8
  7.1 83.8 %shard_map.91 = f32[4,8,2,48,128]{4,3,2,1,0:T(8,128)S(1)} custom-call(s32[8]{0:T(128)S(1)} %copy-done.7, f32[8,8]{1,0:T(8,128)S(1)} %copy-done.3, f32[8,8]{1,0:T(8,128)S(1)} %copy-done.2, f32[2]{0:T(128)S(1)} %copy-done.8, f32[8,2,48,128]{3,2,1,0:T(8,128)S(1)} %copy-done.1, f32[4,8,2,48,128]{4,3,2,1,0:T(8,128)S(1)} %copy-done, s32[4,48]{1,0:T(4,128)S(1)} %copy-done.4, ...), custom_call_target="tpu_custom_call" | custom-call | tf_op jit(solution)/shard_map/pallas_call | solution.py:441
  90.9 1.1 %copy.11 = f32[4,8,2,48,128]{4,3,2,1,0:T(8,128)} copy(f32[4,8,2,48,128]{4,3,2,1,0:T(8,128)S(1)} %shard_map.91) | data formatting | bytes 3145728
Async XLA Ops:
  0.0 1.4 %copy-start = (f32[4,8,2,48,128]{4,3,2,1,0:T(8,128)S(1)}, f32[4,8,2,48,128]{4,3,2,1,0:T(8,128)}, u32[]{:S(2)}) copy-start(f32[4,8,2,48,128]{4,3,2,1,0:T(8,128)} %states_ref.1) | copy-start | bytes 4718596
  1.4 1.0 %copy-start.1 = (f32[8,2,48,128]{3,2,1,0:T(8,128)S(1)}, f32[8,2,48,128]{3,2,1,0:T(8,128)}, u32[]{:S(2)}) copy-start(f32[8,2,48,128]{3,2,1,0:T(8,128)} %init_ref.1) | copy-start | bytes 1179652
  2.4 0.7 copy-start.2
  3.1 0.7 copy-start.3
  3.8 0.7 copy-start.4
  4.5 0.7 copy-start.5
  5.1 0.7 copy-start.6
  5.8 0.7 copy-start.7
  6.5 0.7 copy-start.8

commit v2 on v1

--- a/solution.py
+++ b/solution.py
@@ -162,40 +162,59 @@
 
 MESH = pl.DeviceIdType.MESH
 ROWS = 8
+LAG = 3
+FORWARD_AFTER = 24
 
 
 def sweep_kernel(
+    order_hbm,
+    reaction_hbm,
+    diff_hbm,
+    init_hbm,
+    states_hbm,
+    depth_hbm,
+    offset_hbm,
+    frac_hbm,
+    out_ref,
     order_ref,
-    quad_ref,
     reaction_ref,
     diff_ref,
+    quad_ref,
     init_ref,
     states_ref,
     depth_ref,
     offset_ref,
     frac_ref,
-    out_ref,
     edge,
     part,
     part_in,
     sect,
+    near_out,
     far_out,
+    near_in,
     far_in,
+    ready,
     row_depth,
     row_offset,
     row_frac,
+    load_s,
     edge_s,
     edge_r,
     part_s,
     part_r,
     sect_s,
     sect_r,
+    near_s,
+    near_r,
     far_s,
     far_r,
+    ready_s,
+    ready_r,
 ):
     slots, tracers, _, nlat, cells = states_ref.shape
     blocks = nlat // ROWS
     chunks = 2 * blocks
+    pieces = chunks * slots
     lev = lax.axis_index("lev")
     node = lax.axis_index("node")
     lon = lax.axis_index("lon")
@@ -203,15 +222,46 @@
     par = lon % 2
     mate = half * 2 + (1 - par)
     middle = (lon == 1) | (lon == 2)
+    border = (lon == 0) | (lon == 3)
+
+    loads = [
+        pltpu.make_async_copy(source, target, load_s.at[i])
+        for i, (source, target) in enumerate(
+            (
+                (states_hbm, states_ref),
+                (order_hbm, order_ref),
+                (reaction_hbm, reaction_ref),
+                (diff_hbm, diff_ref),
+                (init_hbm, init_ref),
+                (depth_hbm, depth_ref),
+                (offset_hbm, offset_ref),
+                (frac_hbm, frac_ref),
+            )
+        )
+    ]
+    for load in loads:
+        load.start()
 
     barrier = pltpu.get_barrier_semaphore()
     pl.semaphore_signal(barrier, inc=1, device_id={"lev": 1 - lev}, device_id_type=MESH)
     pl.semaphore_signal(barrier, inc=1, device_id={"node": 1 - node}, device_id_type=MESH)
-    for step in range(1, 4):
-        pl.semaphore_signal(
-            barrier, inc=1, device_id={"lon": (lon + step) % 4}, device_id_type=MESH
-        )
-    pl.semaphore_wait(barrier, 5)
+    pl.semaphore_signal(barrier, inc=1, device_id={"lon": mate}, device_id_type=MESH)
+
+    @pl.when(middle)
+    def _():
+        pl.semaphore_signal(barrier, inc=1, device_id={"lon": 3 - lon}, device_id_type=MESH)
+
+    table = lobatto_table()
+    for m in range(NODES):
+        for n in range(NODES):
+            quad_ref[m, n] = jnp.float32(table[m, n])
+
+    pl.semaphore_wait(barrier, jnp.where(middle, 4, 3))
+
+    def place(c):
+        block = c // 2
+        level = jnp.where(c % 2 == 0, lev, 1 - lev)
+        return block, level, pl.ds(pl.multiple_of(block * ROWS, ROWS), ROWS)
 
     def edge_copy(block):
         rows = pl.ds(pl.multiple_of(block * ROWS, ROWS), ROWS)
@@ -224,59 +274,80 @@
             device_id_type=MESH,
         )
 
-    def part_copy(c):
+    def part_copy(f):
         return pltpu.make_async_remote_copy(
-            src_ref=part.at[c],
-            dst_ref=part_in.at[c],
-            send_sem=part_s.at[c],
-            recv_sem=part_r.at[c],
+            src_ref=part.at[f],
+            dst_ref=part_in.at[f],
+            send_sem=part_s.at[f],
+            recv_sem=part_r.at[f],
             device_id={"node": 1 - node},
             device_id_type=MESH,
         )
 
-    def sect_copy(c):
+    def sect_copy(f):
         return pltpu.make_async_remote_copy(
-            src_ref=sect.at[par, c],
-            dst_ref=sect.at[par, c],
-            send_sem=sect_s.at[c],
-            recv_sem=sect_r.at[c],
+            src_ref=sect.at[par, f],
+            dst_ref=sect.at[par, f],
+            send_sem=sect_s.at[f],
+            recv_sem=sect_r.at[f],
             device_id={"lon": mate},
             device_id_type=MESH,
         )
 
-    def far_copy(which, c):
+    def near_copy(f):
         return pltpu.make_async_remote_copy(
-            src_ref=far_out.at[which, c],
-            dst_ref=far_in.at[c],
-            send_sem=far_s.at[which, c],
-            recv_sem=far_r.at[c],
-            device_id={"lon": (1 - half) * 2 + which},
+            src_ref=near_out.at[f],
+            dst_ref=near_in.at[f],
+            send_sem=near_s.at[f],
+            recv_sem=near_r.at[f],
+            device_id={"lon": 3 - lon},
             device_id_type=MESH,
         )
+
+    def far_copy(f):
+        return pltpu.make_async_remote_copy(
+            src_ref=far_out.at[f],
+            dst_ref=far_in.at[f],
+            send_sem=far_s.at[f],
+            recv_sem=far_r.at[f],
+            device_id={"lon": 3 - lon},
+            device_id_type=MESH,
+        )
+
+    def ready_copy(f):
+        _, level, rows = place(f // slots)
+        return pltpu.make_async_remote_copy(
+            src_ref=ready.at[f],
+            dst_ref=out_ref.at[f % slots, :, level, rows, :],
+            send_sem=ready_s.at[f],
+            recv_sem=ready_r.at[f],
+            device_id={"lon": mate},
+            device_id_type=MESH,
+        )
+
+    loads[0].wait()
 
     def start_edge(block, carry):
         edge_copy(block).start()
         return carry
 
     lax.fori_loop(0, blocks, start_edge, 0)
-
-    diagonal = lax.broadcasted_iota(jnp.int32, (nlat, nlat), 0) == lax.broadcasted_iota(
-        jnp.int32, (nlat, nlat), 1
-    )
-    for a in range(slots):
-        for source, target in (
-            (depth_ref, row_depth),
-            (offset_ref, row_offset),
-            (frac_ref, row_frac),
-        ):
-            line = jnp.broadcast_to(source[a : a + 1, :], (nlat, nlat)).astype(jnp.float32)
-            column = jnp.sum(jnp.where(diagonal, line, 0.0), axis=1, keepdims=True)
-            target[a] = jnp.broadcast_to(column, (nlat, cells)).astype(target.dtype)
-
-    def place(c):
-        block = c // 2
-        level = jnp.where(c % 2 == 0, lev, 1 - lev)
-        return block, level, pl.ds(pl.multiple_of(block * ROWS, ROWS), ROWS)
+    for load in loads[1:]:
+        load.wait()
+
+    def spread_rows():
+        diagonal = lax.broadcasted_iota(jnp.int32, (nlat, nlat), 0) == lax.broadcasted_iota(
+            jnp.int32, (nlat, nlat), 1
+        )
+        for a in range(slots):
+            for source, target in (
+                (depth_ref, row_depth),
+                (offset_ref, row_offset),
+                (frac_ref, row_frac),
+            ):
+                line = jnp.broadcast_to(source[a : a + 1, :], (nlat, nlat)).astype(jnp.float32)
+                column = jnp.sum(jnp.where(diagonal, line, 0.0), axis=1, keepdims=True)
+                target[a] = jnp.broadcast_to(column, (nlat, cells)).astype(target.dtype)
 
     def tendencies(c):
         block, level, rows = place(c)
@@ -303,8 +374,9 @@
                     row.append(value)
                 tend.append(row)
             for target in range(2):
-                group = jnp.where(target == 0, 1 - node, node)
+                group = 1 - node if target == 0 else node
                 for a in range(slots):
+                    f = c * slots + a
                     to = order_ref[group * slots + a]
                     w = [
                         time_step * quad_ref[to, order_ref[node * slots + m]]
@@ -315,103 +387,142 @@
                         for m in range(1, slots):
                             value = value + w[m] * tend[m][t]
                         if target == 0:
-                            part[c, a, t] = value
+                            part[f, t] = value
                         else:
-                            sect[par, c, a, t] = init_ref[t, level, rows, :] + value
+                            sect[par, f, t] = init_ref[t, level, rows, :] + value
+                    if target == 0:
+                        part_copy(f).start()
 
         pl.when(outer)(lambda: body(True))
         pl.when(jnp.logical_not(outer))(lambda: body(False))
-        part_copy(c).start()
-
-    def section(c):
-        part_copy(c).wait_recv()
-        sect[par, c] = sect[par, c] + part_in[c]
-        sect_copy(c).start()
-
-    def interpolate(c):
-        block, level, rows = place(c)
-        sect_copy(c).wait_recv()
+
+    def section(f):
+        part_copy(f).wait_recv()
+        sect[par, f] = sect[par, f] + part_in[f]
+        pl.when(border)(lambda: sect_copy(f).start())
+
+    def interpolate(f):
+        a = f % slots
+        block, level, rows = place(f // slots)
+        sect_copy(f).wait_recv()
         lanes = lax.broadcasted_iota(jnp.int32, (ROWS, cells), 1)
-
-        def per_slot(a, carry):
-            depth = row_depth[a, rows, :]
-            offset = row_offset[a, rows, :]
-            coeffs = cubic_weights(row_frac[a, rows, :])
-            picks = [(lanes - offset + k) & (cells - 1) for k in range(-1, 3)]
-            reach = [
-                jnp.where(lanes >= offset - k, depth, depth + 1) for k in range(-1, 3)
+        depth = row_depth[a, rows, :]
+        offset = row_offset[a, rows, :]
+        coeffs = cubic_weights(row_frac[a, rows, :])
+        picks = [(lanes - offset + k) & (cells - 1) for k in range(-1, 3)]
+        reach = [jnp.where(lanes >= offset - k, depth, depth + 1) for k in range(-1, 3)]
+
+        def weights_of(u):
+            rel = [(u - e) & 3 for e in reach]
+            return [
+                [jnp.where(r == source, w, 0.0) for r, w in zip(rel, coeffs)]
+                for source in range(2)
             ]
 
-            def weights_of(u):
-                rel = [(u - e) & 3 for e in reach]
-                return [
-                    [jnp.where(r == source, w, 0.0) for r, w in zip(rel, coeffs)]
-                    for source in range(2)
+        def total(taps, weights):
+            value = None
+            for source in range(2):
+                for k in range(4):
+                    term = weights[source][k] * taps[source][k]
+                    value = term if value is None else value + term
+            return value
+
+        w_far = weights_of(2 + par)
+        w_near = weights_of(3 - par)
+        w_mate = weights_of(1 - par)
+        w_own = weights_of(par)
+        for t in range(tracers):
+            taps = [
+                [
+                    jnp.take_along_axis(
+                        sect[source, f, t], p, axis=1, mode="promise_in_bounds"
+                    )
+                    for p in picks
                 ]
-
-            def total(taps, weights):
-                value = None
-                for source in range(2):
-                    for k in range(4):
-                        term = weights[source][k] * taps[source][k]
-                        value = term if value is None else value + term
-                return value
-
-            def run(with_far):
-                own = weights_of(par)
-                far = [weights_of(2), weights_of(3)] if with_far else []
-                for t in range(tracers):
-                    fields = [sect[source, c, a, t] for source in range(2)]
-                    taps = [
-                        [
-                            jnp.take_along_axis(f, p, axis=1, mode="promise_in_bounds")
-                            for p in picks
-                        ]
-                        for f in fields
-                    ]
-                    out_ref[a, t, level, rows, :] = total(taps, own)
-                    for which, weights in enumerate(far):
-                        far_out[which, c, a, t] = total(taps, weights)
-
-            pl.when(middle)(lambda: run(True))
-            pl.when(jnp.logical_not(middle))(lambda: run(False))
-            return carry
-
-        lax.fori_loop(0, slots, per_slot, 0)
-
-        @pl.when(middle)
-        def _():
-            far_copy(0, c).start()
-            far_copy(1, c).start()
+                for source in range(2)
+            ]
+            far_out[f, t] = total(taps, w_far)
+            near_out[f, t] = total(taps, w_near)
+            ready[f, t] = total(taps, w_mate)
+            out_ref[a, t, level, rows, :] = total(taps, w_own)
+        far_copy(f).start()
+        near_copy(f).start()
+
+    def forward(f):
+        far_copy(f).wait_recv()
+        ready[f] = ready[f] + far_in[f]
+        ready_copy(f).start()
+
+    def finish(f):
+        _, level, rows = place(f // slots)
+        a = f % slots
+        near_copy(f).wait_recv()
+        out_ref[a, :, level, rows, :] = out_ref[a, :, level, rows, :] + near_in[f]
+
+    tendencies(0)
+    pl.when(middle)(spread_rows)
 
     def step(i, carry):
         pl.when(i < chunks)(lambda: tendencies(i))
-        pl.when((i >= 1) & (i < chunks + 1))(lambda: section(i - 1))
-        pl.when(i >= 2)(lambda: interpolate(i - 2))
+
+        def fine(a, carry):
+            f = (i - 1) * slots + a
+            pl.when(f < pieces)(lambda: section(f))
+
+            @pl.when(middle)
+            def _():
+                g = f - LAG
+                pl.when((g >= 0) & (g < pieces))(lambda: interpolate(g))
+                late = f - FORWARD_AFTER
+                pl.when((late >= 0) & (f % 2 == 0) & (f < pieces))(
+                    lambda: forward(late // 2)
+                )
+
+            return carry
+
+        lax.fori_loop(0, slots, fine, 0)
         return carry
 
-    lax.fori_loop(0, chunks + 2, step, 0)
-
-    def finish(c, carry):
-        block, level, rows = place(c)
-        far_copy(0, c).wait_recv()
-        out_ref[:, :, level, rows, :] = out_ref[:, :, level, rows, :] + far_in[c]
+    lax.fori_loop(1, chunks + 2, step, 0)
+
+    done = (pieces - FORWARD_AFTER + 1) // 2
+
+    @pl.when(middle)
+    def _():
+        def early(f, carry):
+            finish(f)
+            return carry
+
+        def rest(f, carry):
+            forward(f)
+            finish(f)
+            return carry
+
+        lax.fori_loop(0, done, early, 0)
+        lax.fori_loop(done, pieces, rest, 0)
+
+        def drain(f, carry):
+            near_copy(f).wait_send()
+            far_copy(f).wait_send()
+            ready_copy(f).wait_send()
+            return carry
+
+        lax.fori_loop(0, pieces, drain, 0)
+
+    @pl.when(border)
+    def _():
+        def drain(f, carry):
+            sect_copy(f).wait_send()
+            ready_copy(f).wait_recv()
+            return carry
+
+        lax.fori_loop(0, pieces, drain, 0)
+
+    def drain_part(f, carry):
+        part_copy(f).wait_send()
         return carry
 
-    lax.fori_loop(0, chunks, finish, 0)
-
-    def drain(c, carry):
-        part_copy(c).wait_send()
-        sect_copy(c).wait_send()
-
-        @pl.when(middle)
-        def _():
-            far_copy(0, c).wait_send()
-            far_copy(1, c).wait_send()
-
-        return carry
-
-    lax.fori_loop(0, chunks, drain, 0)
+    lax.fori_loop(0, pieces, drain_part, 0)
 
     def drain_edge(block, carry):
         edge_copy(block).wait_send()
@@ -432,42 +543,49 @@
 ):
     slots, tracers, levels, nlat, cells = node_states.shape
     blocks = nlat // ROWS
-    chunks = 2 * blocks
-    piece = (slots, tracers, ROWS, cells)
-    smem = pl.BlockSpec(memory_space=pltpu.SMEM)
-    vmem = pl.BlockSpec(memory_space=pltpu.VMEM)
+    pieces = 2 * blocks * slots
     f32 = jnp.float32
     dma = pltpu.SemaphoreType.DMA
+    smem_of = lambda x: pltpu.SMEM(x.shape, x.dtype)
+    vmem_of = lambda x: pltpu.VMEM(x.shape, x.dtype)
+    pieces_of = lambda *lead: pltpu.VMEM((*lead, pieces, tracers, ROWS, cells), f32)
     return pl.pallas_call(
         sweep_kernel,
         out_shape=jax.ShapeDtypeStruct(node_states.shape, f32),
-        in_specs=[smem] * 4 + [vmem] * 5,
-        out_specs=vmem,
+        in_specs=[pl.BlockSpec(memory_space=pl.ANY)] * 8,
+        out_specs=pl.BlockSpec(memory_space=pltpu.VMEM),
         scratch_shapes=[
+            smem_of(node_order),
+            smem_of(reaction_matrix),
+            smem_of(diffusivity),
+            pltpu.SMEM((NODES, NODES), f32),
+            vmem_of(initial_state),
+            vmem_of(node_states),
+            vmem_of(sector_depth),
+            vmem_of(cell_offset),
+            vmem_of(fraction),
             pltpu.VMEM((slots, tracers, nlat, cells), f32),
-            pltpu.VMEM((chunks, *piece), f32),
-            pltpu.VMEM((chunks, *piece), f32),
-            pltpu.VMEM((2, chunks, *piece), f32),
-            pltpu.VMEM((2, chunks, *piece), f32),
-            pltpu.VMEM((chunks, *piece), f32),
+            pieces_of(),
+            pieces_of(),
+            pieces_of(2),
+            pieces_of(),
+            pieces_of(),
+            pieces_of(),
+            pieces_of(),
+            pieces_of(),
             pltpu.VMEM((slots, nlat, cells), jnp.int32),
             pltpu.VMEM((slots, nlat, cells), jnp.int32),
             pltpu.VMEM((slots, nlat, cells), f32),
+            dma((8,)),
             dma((blocks,)),
             dma((blocks,)),
-            dma((chunks,)),
-            dma((chunks,)),
-            dma((chunks,)),
-            dma((chunks,)),
-            dma((2, chunks)),
-            dma((chunks,)),
-        ],
+        ]
+        + [dma((pieces,))] * 10,
         compiler_params=pltpu.CompilerParams(
-            collective_id=0, has_side_effects=True, vmem_limit_bytes=40 * 1024 * 1024
+            collective_id=0, has_side_effects=True, vmem_limit_bytes=56 * 1024 * 1024
         ),
     )(
         node_order,
-        jnp.asarray(lobatto_table(), f32),
         reaction_matrix,
         diffusivity,
         initial_state,

time: 92.4 us -> 90.2 us (0.976)
  local copies, waits for them, and re-layouts: 8.27 us -> 2.66 us
  Pallas kernels: 83.8 us -> 87.4 us
    unnamed x19 -> x1, local copies, waits for them, and re-layouts: 8.27 us -> 2.66 us
    pallas_call x1, Pallas kernels: 83.8 us -> 87.4 us  [kernel_shards(): pl.pallas_call(sweep_kernel, out_shape=jax.ShapeDtypeStruct(node_states.s...]
where the time goes in v2:
time: 90.2 us; the launch traced here: 90.1 us
  Pallas kernels  87.4 us (97%)
  local copies, waits for them, and re-layouts  2.66 us (3%)
    pallas_call x1, Pallas kernels, kernel_shards(): pl.pallas_call(sweep_kernel, out_shape=jax.ShapeDtypeStruct(node_states.s...  87.4 us
    unnamed x1, local copies, waits for them, and re-layouts  2.66 us

profile of v2, /device:TPU:0, one launch (start us, length us, event | category | flops | bytes accessed | tf_op | source)
XLA Modules:
  0.0 90.1 jit_solution(5791485795946199682)
XLA Ops:
  0.0 87.4 %shard_map.82 = f32[4,8,2,48,128]{4,3,2,1,0:T(8,128)} custom-call(s32[8]{0:T(128)} %order_hbm.1, f32[8,8]{1,0:T(8,128)} %reaction_hbm.1, f32[2]{0:T(128)} %diff_hbm.1, f32[8,2,48,128]{3,2,1,0:T(8,128)} %init_hbm.1, f32[4,8,2,48,128]{4,3,2,1,0:T(8,128)} %states_hbm.1, s32[4,48]{1,0:T(4,128)} %depth_hbm.1, s32[4,48]{1,0:T(4,128)} %offset_hbm.1, f32[4,48]{1,0:T(4,128)} %frac_hbm.1), custom_call_target="tpu_custom_call" | custom-call | tf_op jit(solution)/shard_map/pallas_call | solution.py:552
  87.4 2.7 %copy.10 = f32[4,8,2,48,128]{4,3,2,1,0:T(8,128)} copy(f32[4,8,2,48,128]{4,3,2,1,0:T(8,128)} %shard_map.82) | data formatting | bytes 3145728

commit v3 on v2

--- a/solution.py
+++ b/solution.py
@@ -163,7 +163,8 @@
 MESH = pl.DeviceIdType.MESH
 ROWS = 8
 LAG = 3
-FORWARD_AFTER = 24
+FORWARD_LAG = 12
+NEAR_EVERY = 4
 
 
 def sweep_kernel(
@@ -194,6 +195,7 @@
     near_in,
     far_in,
     ready,
+    result,
     row_depth,
     row_offset,
     row_frac,
@@ -210,6 +212,7 @@
     far_r,
     ready_s,
     ready_r,
+    result_s,
 ):
     slots, tracers, _, nlat, cells = states_ref.shape
     blocks = nlat // ROWS
@@ -403,7 +406,7 @@
 
     def interpolate(f):
         a = f % slots
-        block, level, rows = place(f // slots)
+        _, _, rows = place(f // slots)
         sect_copy(f).wait_recv()
         lanes = lax.broadcasted_iota(jnp.int32, (ROWS, cells), 1)
         depth = row_depth[a, rows, :]
@@ -444,20 +447,25 @@
             far_out[f, t] = total(taps, w_far)
             near_out[f, t] = total(taps, w_near)
             ready[f, t] = total(taps, w_mate)
-            out_ref[a, t, level, rows, :] = total(taps, w_own)
+            result[f, t] = total(taps, w_own)
         far_copy(f).start()
-        near_copy(f).start()
+        pl.when(f % NEAR_EVERY == 0)(lambda: near_copy(f // NEAR_EVERY).start())
 
     def forward(f):
         far_copy(f).wait_recv()
         ready[f] = ready[f] + far_in[f]
         ready_copy(f).start()
 
+    def result_copy(f):
+        _, level, rows = place(f // slots)
+        return pltpu.make_async_copy(
+            result.at[f], out_ref.at[f % slots, :, level, rows, :], result_s.at[f]
+        )
+
     def finish(f):
-        _, level, rows = place(f // slots)
-        a = f % slots
         near_copy(f).wait_recv()
-        out_ref[a, :, level, rows, :] = out_ref[a, :, level, rows, :] + near_in[f]
+        result[f] = result[f] + near_in[f]
+        result_copy(f).start()
 
     tendencies(0)
     pl.when(middle)(spread_rows)
@@ -473,10 +481,8 @@
             def _():
                 g = f - LAG
                 pl.when((g >= 0) & (g < pieces))(lambda: interpolate(g))
-                late = f - FORWARD_AFTER
-                pl.when((late >= 0) & (f % 2 == 0) & (f < pieces))(
-                    lambda: forward(late // 2)
-                )
+                late = f - FORWARD_LAG
+                pl.when((late >= 0) & (f < pieces))(lambda: forward(late))
 
             return carry
 
@@ -485,26 +491,29 @@
 
     lax.fori_loop(1, chunks + 2, step, 0)
 
-    done = (pieces - FORWARD_AFTER + 1) // 2
-
     @pl.when(middle)
     def _():
-        def early(f, carry):
+        def start_near(f, carry):
+            near_copy(f).start()
+            return carry
+
+        def forward_rest(f, carry):
+            forward(f)
+            return carry
+
+        def finish_all(f, carry):
             finish(f)
             return carry
 
-        def rest(f, carry):
-            forward(f)
-            finish(f)
-            return carry
-
-        lax.fori_loop(0, done, early, 0)
-        lax.fori_loop(done, pieces, rest, 0)
+        lax.fori_loop((pieces + NEAR_EVERY - 1) // NEAR_EVERY, pieces, start_near, 0)
+        lax.fori_loop(pieces - FORWARD_LAG, pieces, forward_rest, 0)
+        lax.fori_loop(0, pieces, finish_all, 0)
 
         def drain(f, carry):
             near_copy(f).wait_send()
             far_copy(f).wait_send()
             ready_copy(f).wait_send()
+            result_copy(f).wait()
             return carry
 
         lax.fori_loop(0, pieces, drain, 0)
@@ -553,7 +562,7 @@
         sweep_kernel,
         out_shape=jax.ShapeDtypeStruct(node_states.shape, f32),
         in_specs=[pl.BlockSpec(memory_space=pl.ANY)] * 8,
-        out_specs=pl.BlockSpec(memory_space=pltpu.VMEM),
+        out_specs=pl.BlockSpec(memory_space=pl.ANY),
         scratch_shapes=[
             smem_of(node_order),
             smem_of(reaction_matrix),
@@ -573,6 +582,7 @@
             pieces_of(),
             pieces_of(),
             pieces_of(),
+            pieces_of(),
             pltpu.VMEM((slots, nlat, cells), jnp.int32),
             pltpu.VMEM((slots, nlat, cells), jnp.int32),
             pltpu.VMEM((slots, nlat, cells), f32),
@@ -580,7 +590,7 @@
             dma((blocks,)),
             dma((blocks,)),
         ]
-        + [dma((pieces,))] * 10,
+        + [dma((pieces,))] * 11,
         compiler_params=pltpu.CompilerParams(
             collective_id=0, has_side_effects=True, vmem_limit_bytes=56 * 1024 * 1024
         ),

time: 90.2 us -> 86.6 us (0.960)
  the two profiles are of different devices: /device:TPU:0 before, /device:TPU:8 now
where the time goes in v3:
time: 86.6 us; the launch traced here: 86.5 us
  Pallas kernels  83.8 us (97%)
  local copies, waits for them, and re-layouts  2.66 us (3%)
    pallas_call x1, Pallas kernels, kernel_shards(): pl.pallas_call(sweep_kernel, out_shape=jax.ShapeDtypeStruct(node_states.s...  83.8 us
    unnamed x1, local copies, waits for them, and re-layouts  2.66 us

profile of v3, /device:TPU:8, one launch (start us, length us, event | category | flops | bytes accessed | tf_op | source)
XLA Modules:
  0.0 86.5 jit_solution(8401838308453104674)
XLA Ops:
  0.0 83.8 %shard_map.82 = f32[4,8,2,48,128]{4,3,2,1,0:T(8,128)} custom-call(s32[8]{0:T(128)} %order_hbm.1, f32[8,8]{1,0:T(8,128)} %reaction_hbm.1, f32[2]{0:T(128)} %diff_hbm.1, f32[8,2,48,128]{3,2,1,0:T(8,128)} %init_hbm.1, f32[4,8,2,48,128]{4,3,2,1,0:T(8,128)} %states_hbm.1, s32[4,48]{1,0:T(4,128)} %depth_hbm.1, s32[4,48]{1,0:T(4,128)} %offset_hbm.1, f32[4,48]{1,0:T(4,128)} %frac_hbm.1), custom_call_target="tpu_custom_call" | custom-call | tf_op jit(solution)/shard_map/pallas_call | solution.py:561
  83.8 2.7 %copy.10 = f32[4,8,2,48,128]{4,3,2,1,0:T(8,128)} copy(f32[4,8,2,48,128]{4,3,2,1,0:T(8,128)} %shard_map.82) | data formatting | bytes 3145728
